TPU v7x, 32 devices: a whole 2x2x4 slice. The times are simulated.
32 devices in a mesh: grp: 2 (over y), seq: 16 (over z, x, core).
Axes of the slice: x: 2, y: 2, z: 4, core: 2. Of those that a mesh axis runs over, the one named last changes fastest.
Arguments:
- query_input: bfloat16 [4096, 4096], P(('grp', 'seq')), parts along dimension 0, may hold values from -6 to 6
- key_input: bfloat16 [4096, 4096], P(('grp', 'seq')), parts along dimension 0, may hold values from -6 to 6
- value_input: bfloat16 [4096, 4096], P(('grp', 'seq')), parts along dimension 0, may hold values from -6 to 6
- output_grad: bfloat16 [4096, 4096], P(('grp', 'seq')), parts along dimension 0, may hold values from -6 to 6
- short_taps: float32 [3, 7, 4096], replicated, may hold values from -2 to 2
- long_filter: bfloat16 [128, 256], replicated, may hold values from -0.5 to 0.5
- skip_gain: float32 [4096], replicated, may hold values from 0.1 to 1.9
- genome_ids: int32 [4096], P('grp'), parts along dimension 0, may hold values from 0 to 7, never falling along the last dimension, each value on 1 to 512 neighbouring positions
Outputs:
- section_out: bfloat16 [4096, 4096], P(('grp', 'seq')), parts along dimension 0
- grad_query: bfloat16 [4096, 4096], P(('grp', 'seq')), parts along dimension 0
- grad_key: bfloat16 [4096, 4096], P(('grp', 'seq')), parts along dimension 0
- grad_value: bfloat16 [4096, 4096], P(('grp', 'seq')), parts along dimension 0
- filter_grad: float32 [256, 256], P('grp'), parts along dimension 0
There are 2 independent parts, one for each index of `grp`. A program takes and returns all parts, laid end to end along the dimension named above; an argument that names none is the same for every part. Nothing has to cross between parts.
Inputs may be any that keep to these rules, and one draw needn't show every extreme that they name: `genome_ids`: genome ids never fall from one row to the next; each genome covers 1 to 512 rows, one exactly 512.
All inputs are finite; a program needn't handle non-finite values.
Results may differ from a plain program's by a relative error of at most 0.0058.
Values may be sent and summed in bfloat16 or wider, within the bound.
A program may use at most 128 MiB of HBM per device.

v0:
```python
import math

import jax
import jax.numpy as jnp
from jax import lax
from jax.sharding import PartitionSpec as P


def short_forward(extended, weights, seg_source, seg_target):
    short_reach = weights.shape[0] - 1
    length = extended.shape[1] - short_reach
    result = jnp.zeros((extended.shape[0], length), jnp.float32)
    for offset in range(short_reach + 1):
        first_row = short_reach - offset
        piece = extended[:, first_row : first_row + length].astype(jnp.float32)
        same_genome = (seg_source[first_row : first_row + length] == seg_target)[None, :]
        result = result + weights[offset][:, None] * jnp.where(
            same_genome, piece, jnp.zeros_like(piece)
        )
    return result


def short_backward(extended, weights, seg_source, seg_target):
    short_reach = weights.shape[0] - 1
    length = extended.shape[1] - short_reach
    result = jnp.zeros((extended.shape[0], length), jnp.float32)
    for offset in range(short_reach + 1):
        piece = extended[:, offset : offset + length].astype(jnp.float32)
        same_genome = (seg_source[offset : offset + length] == seg_target)[None, :]
        result = result + weights[offset][:, None] * jnp.where(
            same_genome, piece, jnp.zeros_like(piece)
        )
    return result


def make_windows(extended, tap_count):
    length = extended.shape[-1] - tap_count
    blocks = length // tap_count
    leading = extended.shape[:-1]
    return jnp.concatenate(
        [
            extended[..., :length].reshape(leading + (blocks, tap_count)),
            extended[..., tap_count:].reshape(leading + (blocks, tap_count)),
        ],
        axis=-1,
    )


def to_units(windows, group_blocks, group_per, group_width, turns, per_turn):
    width = windows.shape[-1]
    shaped = windows.reshape(group_blocks, group_per, group_width, turns, per_turn, width)
    return shaped.transpose(3, 0, 1, 2, 4, 5).reshape(
        turns * group_blocks, group_per, group_width, per_turn, width
    )


def seg_units(seg_rows, turns, group_blocks, per_turn):
    width = seg_rows.shape[-1]
    shaped = seg_rows.reshape(turns, 1, per_turn, width)
    return jnp.broadcast_to(shaped, (turns, group_blocks, per_turn, width)).reshape(
        turns * group_blocks, per_turn, width
    )


def toeplitz_table(long_filter, forward):
    tap_count, group_count = long_filter.shape
    rows = long_filter.T
    if forward:
        base = jnp.concatenate(
            [
                jnp.zeros((group_count, 1), rows.dtype),
                rows[:, ::-1],
                jnp.zeros((group_count, tap_count), rows.dtype),
            ],
            axis=1,
        )
    else:
        base = jnp.concatenate([rows, jnp.zeros((group_count, tap_count + 1), rows.dtype)], axis=1)
    tiled = jnp.tile(base, (1, tap_count))[:, : tap_count * 2 * tap_count]
    return tiled.reshape(group_count, tap_count, 2 * tap_count)


def grouped_conv(extended, seg_ext, long_filter, forward, per_turn, group_per):
    tap_count, group_count = long_filter.shape
    channels = extended.shape[0]
    length = extended.shape[1] - tap_count
    group_width = channels // group_count
    turns = length // tap_count // per_turn
    group_blocks = group_count // group_per
    units = turns * group_blocks
    windows = to_units(
        make_windows(extended, tap_count), group_blocks, group_per, group_width, turns, per_turn
    )
    seg_windows = seg_units(make_windows(seg_ext, tap_count), turns, group_blocks, per_turn)
    if forward:
        target_rows = seg_ext[tap_count:]
    else:
        target_rows = seg_ext[:length]
    seg_targets = seg_units(
        target_rows.reshape(turns * per_turn, tap_count), turns, group_blocks, per_turn
    )
    table = toeplitz_table(long_filter, forward).reshape(
        group_blocks, group_per, tap_count, 2 * tap_count
    )
    table = jnp.broadcast_to(
        table[None], (turns, group_blocks, group_per, tap_count, 2 * tap_count)
    )
    table = table.reshape(units, group_per, tap_count, 2 * tap_count)

    def grouped_one_unit(inputs):
        block_rows, seg_source, seg_target, unit_table = inputs
        same_genome = (seg_target[:, :, None] == seg_source[:, None, :]).astype(unit_table.dtype)
        masked = unit_table[None] * same_genome[:, None]
        return jnp.einsum("kgts,gcks->gckt", masked, block_rows, preferred_element_type=jnp.float32)

    result = lax.map(grouped_one_unit, (windows, seg_windows, seg_targets, table))
    result = result.reshape(turns, group_blocks, group_per, group_width, per_turn, tap_count)
    return result.transpose(1, 2, 3, 0, 4, 5).reshape(channels, length)


def filter_terms(conv_grad, extended, seg_ext, tap_count, group_count, per_turn, group_per):
    channels, length = conv_grad.shape
    group_width = channels // group_count
    blocks = length // tap_count
    turns = blocks // per_turn
    group_blocks = group_count // group_per
    values = to_units(
        make_windows(extended, tap_count), group_blocks, group_per, group_width, turns, per_turn
    )
    grads = to_units(
        conv_grad.reshape(channels, blocks, tap_count),
        group_blocks,
        group_per,
        group_width,
        turns,
        per_turn,
    )
    seg_windows = seg_units(make_windows(seg_ext, tap_count), turns, group_blocks, per_turn)
    seg_targets = seg_units(
        seg_ext[tap_count:].reshape(blocks, tap_count), turns, group_blocks, per_turn
    )
    target = jnp.arange(tap_count, dtype=jnp.int32)[:, None, None]
    source = jnp.arange(2 * tap_count, dtype=jnp.int32)[None, :, None]
    lag_index = jnp.arange(tap_count, dtype=jnp.int32)[None, None, :]
    selector = (tap_count + target - source == lag_index).astype(jnp.float32)

    def filter_one_unit(inputs):
        grad_rows, value_rows, seg_source, seg_target = inputs
        same_genome = (seg_target[:, :, None] == seg_source[:, None, :]).astype(jnp.float32)
        products = (
            jnp.einsum("gckt,gcks->kgts", grad_rows, value_rows, preferred_element_type=jnp.float32)
            * same_genome[:, None]
        )
        collected = jnp.sum(products, axis=0)
        return jnp.einsum("gts,tsj->jg", collected, selector, precision=lax.Precision.HIGHEST)

    terms = lax.map(filter_one_unit, (grads, values, seg_windows, seg_targets))
    terms = jnp.sum(terms.reshape(turns, group_blocks, tap_count, group_per), axis=0)
    return terms.transpose(1, 0, 2).reshape(tap_count, group_count)


def conv_section(
    query_input,
    key_input,
    value_input,
    output_grad,
    short_weights,
    long_filter,
    skip_gain,
    seg_front,
    seg_back,
    per_turn,
    group_per,
    fetch_short,
    fetch_long,
    fetch_grad,
    fetch_back,
):
    length = query_input.shape[1]
    tap_count, group_count = long_filter.shape
    short_reach = short_weights.shape[1] - 1
    seg_own = seg_front[tap_count:]
    short_source = seg_front[tap_count - short_reach :]
    back_source = seg_back[: length + short_reach]
    rim_query, rim_key, rim_value = fetch_short(
        query_input[:, length - short_reach :],
        key_input[:, length - short_reach :],
        value_input[:, length - short_reach :],
    )
    query_short = short_forward(
        jnp.concatenate([rim_query, query_input], 1), short_weights[0], short_source, seg_own
    )
    key_short = short_forward(
        jnp.concatenate([rim_key, key_input], 1), short_weights[1], short_source, seg_own
    )
    value_short = short_forward(
        jnp.concatenate([rim_value, value_input], 1), short_weights[2], short_source, seg_own
    )
    gated_pair = (key_short * value_short).astype(jnp.bfloat16)
    extended = jnp.concatenate([fetch_long(gated_pair[:, length - tap_count :]), gated_pair], 1)
    conv_out = grouped_conv(
        extended, seg_front, long_filter, True, per_turn, group_per
    ) + skip_gain[:, None] * gated_pair.astype(jnp.float32)
    section_out = (query_short * conv_out).astype(jnp.bfloat16)
    cotangent = output_grad.astype(jnp.float32)
    conv_grad = (cotangent * query_short).astype(jnp.bfloat16)
    query_grad_short = (cotangent * conv_out).astype(jnp.bfloat16)
    grad_ext = jnp.concatenate([conv_grad, fetch_grad(conv_grad[:, :tap_count])], 1)
    pair_grad = grouped_conv(
        grad_ext, seg_back, long_filter, False, per_turn, group_per
    ) + skip_gain[:, None] * conv_grad.astype(jnp.float32)
    key_grad_short = (pair_grad * value_short).astype(jnp.bfloat16)
    value_grad_short = (pair_grad * key_short).astype(jnp.bfloat16)
    back_query, back_key, back_value = fetch_back(
        query_grad_short[:, :short_reach],
        key_grad_short[:, :short_reach],
        value_grad_short[:, :short_reach],
    )
    grad_query = short_backward(
        jnp.concatenate([query_grad_short, back_query], 1), short_weights[0], back_source, seg_own
    ).astype(jnp.bfloat16)
    grad_key = short_backward(
        jnp.concatenate([key_grad_short, back_key], 1), short_weights[1], back_source, seg_own
    ).astype(jnp.bfloat16)
    grad_value = short_backward(
        jnp.concatenate([value_grad_short, back_value], 1), short_weights[2], back_source, seg_own
    ).astype(jnp.bfloat16)
    partial_terms = filter_terms(
        conv_grad, extended, seg_front, tap_count, group_count, per_turn, group_per
    )
    return (section_out, grad_query, grad_key, grad_value, partial_terms)


def zero_three(first, second, third):
    return (jnp.zeros_like(first), jnp.zeros_like(second), jnp.zeros_like(third))


def zero_one(piece):
    return jnp.zeros_like(piece)


def body(
    query_input, key_input, value_input, output_grad, short_taps, long_filter, skip_gain, genome_ids
):
    row_count, channels = query_input.shape
    tap_count, group_count = long_filter.shape
    group_width = channels // group_count
    seq_count = lax.axis_size("seq")
    seq_index = lax.axis_index("seq")
    scale = 1.0 / math.sqrt(group_width * row_count * seq_count)
    seg_pad = jnp.pad(genome_ids, (tap_count, tap_count), constant_values=-1)
    unit_limit = 2**22
    local_width = channels // seq_count
    local_groups = local_width // group_width
    total_rows = row_count * seq_count
    moved_query, moved_key, moved_value, moved_grad = (
        lax.all_to_all(query_input.T, "seq", split_axis=0, concat_axis=1, tiled=True),
        lax.all_to_all(key_input.T, "seq", split_axis=0, concat_axis=1, tiled=True),
        lax.all_to_all(value_input.T, "seq", split_axis=0, concat_axis=1, tiled=True),
        lax.all_to_all(output_grad.T, "seq", split_axis=0, concat_axis=1, tiled=True),
    )
    local_short = lax.dynamic_slice_in_dim(short_taps, seq_index * local_width, local_width, 2)
    local_filter = lax.dynamic_slice_in_dim(long_filter, seq_index * local_groups, local_groups, 1)
    local_gain = lax.dynamic_slice_in_dim(skip_gain, seq_index * local_width, local_width, 0)
    seg_front = seg_pad[: total_rows + tap_count]
    seg_back = seg_pad[tap_count:]
    per_turn = math.gcd(total_rows // tap_count, 64)
    group_per = math.gcd(local_groups, max(1, unit_limit // (per_turn * 2 * tap_count * tap_count)))
    section_out, grad_query, grad_key, grad_value, partial_terms = conv_section(
        moved_query,
        moved_key,
        moved_value,
        moved_grad,
        local_short,
        local_filter,
        local_gain,
        seg_front,
        seg_back,
        per_turn,
        group_per,
        zero_three,
        zero_one,
        zero_one,
        zero_three,
    )
    filter_grad = lax.all_gather(partial_terms * scale, "seq", axis=1, tiled=True)
    section_out, grad_query, grad_key, grad_value = (
        lax.all_to_all(section_out, "seq", split_axis=1, concat_axis=0, tiled=True),
        lax.all_to_all(grad_query, "seq", split_axis=1, concat_axis=0, tiled=True),
        lax.all_to_all(grad_key, "seq", split_axis=1, concat_axis=0, tiled=True),
        lax.all_to_all(grad_value, "seq", split_axis=1, concat_axis=0, tiled=True),
    )
    return (section_out.T, grad_query.T, grad_key.T, grad_value.T, filter_grad)


def solution(mesh):
    return jax.shard_map(
        body,
        mesh=mesh,
        in_specs=(
            P(("grp", "seq"), None),
            P(("grp", "seq"), None),
            P(("grp", "seq"), None),
            P(("grp", "seq"), None),
            P(),
            P(),
            P(),
            P("grp"),
        ),
        out_specs=(
            P(("grp", "seq"), None),
            P(("grp", "seq"), None),
            P(("grp", "seq"), None),
            P(("grp", "seq"), None),
            P("grp", None),
        ),
        check_vma=False,
    )
```

profile of v0, /device:TPU:0, one launch (start us, length us, event | category | flops | bytes accessed | tf_op | source)
XLA Modules:
  0.0 329.5 jit_solution(375717648918043440)
XLA Ops:
  3.0 7.4 %all-to-all-start.4 = ((bf16[16,256,128]{2,1,0:T(8,128)(2,1)}), bf16[16,256,128]{2,1,0:T(8,128)(2,1)S(1)}, u32[]{:S(2)}, u32[]{:S(2)}) async-start(bf16[16,256,128]{2,1,0:T(8,128)(2,1)} %bitcast.51), calls=%async_computation.4 | async-start | bytes 2097152 | tf_op jit(solution)/shard_map/all_to_all | solution.py:260
  11.7 21.6 %all-to-all-done.4 = bf16[16,256,128]{2,1,0:T(8,128)(2,1)S(1)} async-done(((bf16[16,256,128]{2,1,0:T(8,128)(2,1)}), bf16[16,256,128]{2,1,0:T(8,128)(2,1)S(1)}, u32[]{:S(2)}, u32[]{:S(2)}) %all-to-all-start.4) | async-done | bytes 1048608 | tf_op jit(solution)/shard_map/all_to_all | solution.py:260
  33.3 6.9 %all-to-all-start = ((bf16[16,256,128]{2,1,0:T(8,128)(2,1)}), bf16[16,256,128]{2,1,0:T(8,128)(2,1)S(1)}, u32[]{:S(2)}, u32[]{:S(2)}) async-start(bf16[16,256,128]{2,1,0:T(8,128)(2,1)} %bitcast.211), calls=%async_computation | async-start | bytes 2097152 | tf_op jit(solution)/shard_map/all_to_all | solution.py:257
  42.9 20.2 %all-to-all-done = bf16[16,256,128]{2,1,0:T(8,128)(2,1)S(1)} async-done(((bf16[16,256,128]{2,1,0:T(8,128)(2,1)}), bf16[16,256,128]{2,1,0:T(8,128)(2,1)S(1)}, u32[]{:S(2)}, u32[]{:S(2)}) %all-to-all-start) | async-done | bytes 1048608 | tf_op jit(solution)/shard_map/all_to_all | solution.py:257
  63.1 6.9 %all-to-all-start.2 = ((bf16[16,256,128]{2,1,0:T(8,128)(2,1)}), bf16[16,256,128]{2,1,0:T(8,128)(2,1)}, u32[]{:S(2)}, u32[]{:S(2)}) async-start(bf16[16,256,128]{2,1,0:T(8,128)(2,1)} %bitcast.34), calls=%async_computation.2 | async-start | bytes 2097152 | tf_op jit(solution)/shard_map/all_to_all | solution.py:259
  71.4 3.1 tile.21
  74.5 2.6 copy.71
  78.5 3.1 tile.9
  83.9 4.5 %fusion.32 = (bf16[256,2048]{1,0:T(8,128)(2,1)S(1)}, f32[256,2048]{1,0:T(8,128)}) fusion(pred[2048]{0:T(1024)(128)(4,1)S(1)} %get-tuple-element.274, f32[256]{0:T(256)S(1)} %bitcast.258, pred[2048]{0:T(1024)(128)(4,1)S(1)} %get-tuple-element.275, f32[256]{0:T(256)S(1)} %bitcast.260, pred[2048]{0:T(1024)(128)(4,1)S(1)} %get-tuple-element.276, ...), kind=kLoop, calls=%fused_computation.48 | loop fusion | flops 15204352 | bytes 5262336 | tf_op jit(solution)/shard_map/convert_element_type | solution.py:206
  93.1 7.1 %all-to-all-start.1 = ((bf16[16,256,128]{2,1,0:T(8,128)(2,1)}), bf16[16,256,128]{2,1,0:T(8,128)(2,1)}, u32[]{:S(2)}, u32[]{:S(2)}) async-start(bf16[16,256,128]{2,1,0:T(8,128)(2,1)} %bitcast.209), calls=%async_computation.1 | async-start | bytes 2097152 | tf_op jit(solution)/shard_map/all_to_all | solution.py:258
  101.7 11.2 %while.32 = (s32[]{:T(128)}, f32[2,8,16,16,128]{4,3,2,1,0:T(8,128)}, bf16[2,8,16,16,256]{4,2,3,1,0:T(8,128)(2,1)}, bf16[2,8,128,256]{3,1,2,0:T(8,128)(2,1)S(1)},...) while((s32[]{:T(128)}, f32[2,8,16,16,128]{4,3,2,1,0:T(8,128)}, ...), condition=%wide.region_3.4_spmd, body=%wide.region_2.3_spmd.sunk | while | flops 139460608 | bytes 25764528 | solution.py:116
  114.3 6.2 %multiply_convert_fusion.1 = (bf16[256,2048]{1,0:T(8,128)(2,1)}, f32[256,2048]{1,0:T(8,128)}) fusion(bf16[256,2048]{1,0:T(8,128)(2,1)S(1)} %get-tuple-element.245, f32[32,8,16,128]{3,2,1,0:T(8,128)} %bitcast.110, f32[256]{0:T(256)S(1)} %dynamic_slice.52, pred[2048]{0:T(1024)(128)(4,1)S(1)} %get-tuple-element.274, f32[256]{0:T(256)S(1)} %bitcast.242, ...), kind=kLoop, calls=%fused_computation.54 | loop fusion | flops 16252928 | bytes 7360512 | tf_op jit(solution)/shard_map/convert_element_type | solution.py:212
  120.5 2.6 all-to-all-done.1
  124.5 6.0 %multiply_convert_fusion = (bf16[256,2048]{1,0:T(8,128)(2,1)}, f32[256,2048]{1,0:T(8,128)S(1)}) fusion(bf16[256,2048]{1,0:T(8,128)(2,1)S(1)} %get-tuple-element.245, f32[32,8,16,128]{3,2,1,0:T(8,128)} %bitcast.110, f32[256]{0:T(256)S(1)} %dynamic_slice.52, pred[2048]{0:T(1024)(128)(4,1)S(1)} %get-tuple-element.274, f32[256]{0:T(256)S(1)} %bitcast.244, ...), kind=kLoop, calls=%fused_computation.52 | loop fusion | flops 16252928 | bytes 7360512 | tf_op jit(solution)/shard_map/convert_element_type | solution.py:213
  134.3 11.2 %while.31 = (s32[]{:T(128)}, f32[2,8,16,16,128]{4,3,2,1,0:T(8,128)}, bf16[2,8,16,16,256]{4,2,1,3,0:T(8,128)(2,1)}, bf16[2,8,128,256]{3,1,2,0:T(8,128)(2,1)S(1)},...) while((s32[]{:T(128)}, f32[2,8,16,16,128]{4,3,2,1,0:T(8,128)}, ...), condition=%wide.region_1.2_spmd, body=%wide.region_0.1_spmd.sunk | while | flops 139460608 | bytes 25764528 | solution.py:116
  145.5 3.8 %fusion.31 = (bf16[256,2048]{1,0:T(8,128)(2,1)S(1)}, bf16[256,2048]{1,0:T(8,128)(2,1)S(1)}) fusion(bf16[256,2048]{1,0:T(8,128)(2,1)S(1)} %multiply_convert_fusion.3, f32[32,8,16,128]{3,2,1,0:T(8,128)} %bitcast.101, f32[256]{0:T(256)S(1)} %dynamic_slice.52, f32[256,2048]{1,0:T(8,128)} %get-tuple-element.246, bf16[16,256,128]{2,1,0:T(8,128)(2,1)} %copy-done.8), kind=kLoop, calls=%fused_computation.47 | loop fusion | flops 4194304 | bytes 8389632 | tf_op jit(solution)/shard_map/convert_element_type | solution.py:207
  149.3 3.3 add_convert_fusion.2
  153.9 6.9 %all-to-all-start.5 = ((bf16[256,16,128]{0,2,1:T(8,128)(2,1)}), bf16[256,16,128]{0,2,1:T(8,128)(2,1)}, u32[]{:S(2)}, u32[]{:S(2)}) async-start(bf16[256,16,128]{0,2,1:T(8,128)(2,1)} %bitcast.214), calls=%async_computation.5 | async-start | bytes 2097152 | tf_op jit(solution)/shard_map/all_to_all | solution.py:289
  162.2 21.7 %all-to-all-done.5 = bf16[256,16,128]{0,2,1:T(8,128)(2,1)} async-done(((bf16[256,16,128]{0,2,1:T(8,128)(2,1)}), bf16[256,16,128]{0,2,1:T(8,128)(2,1)}, u32[]{:S(2)}, u32[]{:S(2)}) %all-to-all-start.5) | async-done | bytes 1048608 | tf_op jit(solution)/shard_map/all_to_all | solution.py:289
  183.8 6.9 %all-to-all-start.3 = ((bf16[256,16,128]{0,2,1:T(8,128)(2,1)}), bf16[256,16,128]{0,2,1:T(8,128)(2,1)S(1)}, u32[]{:S(2)}, u32[]{:S(2)}) async-start(bf16[256,16,128]{0,2,1:T(8,128)(2,1)} %bitcast.213), calls=%async_computation.3 | async-start | bytes 2097152 | tf_op jit(solution)/shard_map/all_to_all | solution.py:288
  190.7 4.1 %add_convert_fusion.1 = bf16[256,2048]{1,0:T(8,128)(2,1)} fusion(bf16[256,2048]{1,0:T(8,128)(2,1)S(1)} %copy-done.11, f32[256]{0:T(256)S(1)} %bitcast.245, f32[256]{0:T(256)S(1)} %bitcast.247, f32[256]{0:T(256)S(1)} %bitcast.249, f32[256]{0:T(256)S(1)} %bitcast.251, f32[256]{0:T(256)S(1)} %bitcast.253, f32[256]{0:T(256)S(1)} %bitcast.255, ...), kind=kLoop, calls=%fused_computation.53 | loop fusion | flops 14155776 | bytes 2116608 | tf_op jit(solution)/shard_map/convert_element_type | solution.py:224
  197.1 16.5 %all-to-all-done.3 = bf16[256,16,128]{0,2,1:T(8,128)(2,1)S(1)} async-done(((bf16[256,16,128]{0,2,1:T(8,128)(2,1)}), bf16[256,16,128]{0,2,1:T(8,128)(2,1)S(1)}, u32[]{:S(2)}, u32[]{:S(2)}) %all-to-all-start.3) | async-done | bytes 1048608 | tf_op jit(solution)/shard_map/all_to_all | solution.py:288
  213.6 6.9 %all-to-all-start.6 = ((bf16[256,16,128]{0,2,1:T(8,128)(2,1)}), bf16[256,16,128]{0,2,1:T(8,128)(2,1)}, u32[]{:S(2)}, u32[]{:S(2)}) async-start(bf16[256,16,128]{0,2,1:T(8,128)(2,1)} %bitcast.212), calls=%async_computation.6 | async-start | bytes 2097152 | tf_op jit(solution)/shard_map/all_to_all | solution.py:290
  220.6 4.1 %add_convert_fusion = bf16[256,2048]{1,0:T(8,128)(2,1)} fusion(bf16[256,2048]{1,0:T(8,128)(2,1)S(1)} %copy-done.10, f32[256]{0:T(256)S(1)} %bitcast.243, f32[256]{0:T(256)S(1)} %bitcast.233, f32[256]{0:T(256)S(1)} %bitcast.235, f32[256]{0:T(256)S(1)} %bitcast.237, f32[256]{0:T(256)S(1)} %bitcast.239, f32[256]{0:T(256)S(1)} %bitcast.241, ...), kind=kLoop, calls=%fused_computation.51 | loop fusion | flops 14155776 | bytes 2116608 | tf_op jit(solution)/shard_map/convert_element_type | solution.py:227
  227.0 16.6 %all-to-all-done.6 = bf16[256,16,128]{0,2,1:T(8,128)(2,1)} async-done(((bf16[256,16,128]{0,2,1:T(8,128)(2,1)}), bf16[256,16,128]{0,2,1:T(8,128)(2,1)}, u32[]{:S(2)}, u32[]{:S(2)}) %all-to-all-start.6) | async-done | bytes 1048608 | tf_op jit(solution)/shard_map/all_to_all | solution.py:290
  243.6 6.9 %all-to-all-start.7 = ((bf16[256,16,128]{0,2,1:T(8,128)(2,1)}), bf16[256,16,128]{0,2,1:T(8,128)(2,1)}, u32[]{:S(2)}, u32[]{:S(2)}) async-start(bf16[256,16,128]{0,2,1:T(8,128)(2,1)} %bitcast.63), calls=%async_computation.7 | async-start | bytes 2097152 | tf_op jit(solution)/shard_map/all_to_all | solution.py:291
  250.5 45.3 %while.33 = (s32[]{:T(128)}, f32[2,128,8]{1,2,0:T(8,128)S(1)}, bf16[2,8,16,16,128]{4,3,2,1,0:T(8,128)(2,1)S(1)}, bf16[2,8,16,16,256]{4,2,1,3,0:T(8,128)(2,1)}, s...) while((s32[]{:T(128)}, f32[2,128,8]{1,2,0:T(8,128)S(1)}, ...), condition=%wide.region_6.7_spmd.clone, body=%wide.region_4.6_spmd.clone.sunk | while | flops 554434560 | bytes 19607684 | solution.py:157
  252.1 2.6 multiply_reduce_fusion.2
  255.1 18.0 %fusion.70 = f32[2,128,8]{1,2,0:T(8,128)S(1)} fusion(f32[2,128,8]{1,2,0:T(8,128)S(1)} %get-tuple-element.454, s32[]{:T(128)} %get-tuple-element.453, f32[8,128,256]{1,0,2:T(8,128)S(1)} %copy.160, s32[128,256]{0,1:T(8,128)S(1)} %get-tuple-element.467), kind=kOutput, calls=%fused_computation.35.clone.1 | convolution fusion | flops 411041792 | bytes 1183748 | tf_op jit(solution)/shard_map/while/body/eval_jaxpr/gts,tsj->jg/dot_general | solution.py:155
  274.8 2.6 multiply_reduce_fusion.2
  277.8 18.0 %fusion.70 = f32[2,128,8]{1,2,0:T(8,128)S(1)} fusion(f32[2,128,8]{1,2,0:T(8,128)S(1)} %get-tuple-element.454, s32[]{:T(128)} %get-tuple-element.453, f32[8,128,256]{1,0,2:T(8,128)S(1)} %copy.160, s32[128,256]{0,1:T(8,128)S(1)} %get-tuple-element.467), kind=kOutput, calls=%fused_computation.35.clone.1 | convolution fusion | flops 411041792 | bytes 1183748 | tf_op jit(solution)/shard_map/while/body/eval_jaxpr/gts,tsj->jg/dot_general | solution.py:155
  295.8 22.0 %all_gather.3 = f32[128,256]{0,1:T(8,128)S(1)} all-gather(f32[128,16]{0,1:T(8,128)S(1)} %multiply_bitcast_fusion), channel_id=1, replica_groups=mesh['grp'=2,'seq'=16] {'seq'}, dimensions={1}, use_global_device_ids=true | all-gather | bytes 139264 | tf_op jit(solution)/shard_map/all_gather | solution.py:286
  (153 shorter events, 69.0 us)
Async XLA Ops:
  0.6 39.6 %copy-start = (bf16[128,256]{1,0:T(8,128)(2,1)S(1)}, bf16[128,256]{1,0:T(8,128)(2,1)}, u32[]{:S(2)}) copy-start(bf16[128,256]{1,0:T(8,128)(2,1)} %param.19) | copy-start | bytes 196612
  0.6 9.7 %copy-start.15 = (bf16[128,4096]{1,0:T(8,128)(2,1)S(1)}, bf16[128,4096]{1,0:T(8,128)(2,1)}, u32[]{:S(2)}) copy-start(bf16[128,4096]{1,0:T(8,128)(2,1)} %param.14) | copy-start | bytes 3145732
  3.0 30.3 %all-to-all-start.4 = ((bf16[16,256,128]{2,1,0:T(8,128)(2,1)}), bf16[16,256,128]{2,1,0:T(8,128)(2,1)S(1)}, u32[]{:S(2)}, u32[]{:S(2)}) async-start(bf16[16,256,128]{2,1,0:T(8,128)(2,1)} %bitcast.51), calls=%async_computation.4 | async-start | bytes 2097152 | tf_op jit(solution)/shard_map/all_to_all | solution.py:260
  33.3 50.6 %copy-start.8 = (bf16[16,256,128]{2,1,0:T(8,128)(2,1)}, bf16[16,256,128]{2,1,0:T(8,128)(2,1)S(1)}, u32[]{:S(2)}) copy-start(bf16[16,256,128]{2,1,0:T(8,128)(2,1)S(1)} %all-to-all-done.4) | copy-start | bytes 3145732
  33.3 29.8 %all-to-all-start = ((bf16[16,256,128]{2,1,0:T(8,128)(2,1)}), bf16[16,256,128]{2,1,0:T(8,128)(2,1)S(1)}, u32[]{:S(2)}, u32[]{:S(2)}) async-start(bf16[16,256,128]{2,1,0:T(8,128)(2,1)} %bitcast.211), calls=%async_computation | async-start | bytes 2097152 | tf_op jit(solution)/shard_map/all_to_all | solution.py:257
  40.4 29.7 %copy-start.19 = (s32[2048]{0:T(1024)S(1)}, s32[2048]{0:T(1024)}, u32[]{:S(2)}) copy-start(s32[2048]{0:T(1024)} %param.21) | copy-start | bytes 24580
  63.1 29.9 %all-to-all-start.2 = ((bf16[16,256,128]{2,1,0:T(8,128)(2,1)}), bf16[16,256,128]{2,1,0:T(8,128)(2,1)}, u32[]{:S(2)}, u32[]{:S(2)}) async-start(bf16[16,256,128]{2,1,0:T(8,128)(2,1)} %bitcast.34), calls=%async_computation.2 | async-start | bytes 2097152 | tf_op jit(solution)/shard_map/all_to_all | solution.py:259
  74.5 2.7 copy-start.5
  81.5 2.4 copy-start.2
  93.1 8.7 %slice-start.1 = ((bf16[16,32896]{1,0:T(8,128)(2,1)}), bf16[16,32768]{1,0:T(8,128)(2,1)S(1)}, s32[]{:S(2)}) async-start(bf16[16,32896]{1,0:T(8,128)(2,1)} %copy-done.5), calls=%async_computation.9 | async-start | bytes 2097152 | tf_op jit(solution)/shard_map/slice | solution.py:79
  93.1 30.1 %all-to-all-start.1 = ((bf16[16,256,128]{2,1,0:T(8,128)(2,1)}), bf16[16,256,128]{2,1,0:T(8,128)(2,1)}, u32[]{:S(2)}, u32[]{:S(2)}) async-start(bf16[16,256,128]{2,1,0:T(8,128)(2,1)} %bitcast.209), calls=%async_computation.1 | async-start | bytes 2097152 | tf_op jit(solution)/shard_map/all_to_all | solution.py:258
  101.7 2.0 copy-start.14
  106.0 1.3 copy-start.7
  107.3 2.0 copy-start.14
  124.5 6.0 %copy-start.9 = (f32[256,2048]{1,0:T(8,128)S(1)}, f32[256,2048]{1,0:T(8,128)}, u32[]{:S(2)}) copy-start(f32[256,2048]{1,0:T(8,128)} %get-tuple-element.244) | copy-start | bytes 6291460
  131.8 2.5 slice-start
  132.2 2.0 copy-start.16
  134.3 2.0 copy-start.17
  138.6 1.3 copy-start.4
  139.9 2.0 copy-start.17
  144.2 1.3 copy-start.4
  153.9 29.9 %all-to-all-start.5 = ((bf16[256,16,128]{0,2,1:T(8,128)(2,1)}), bf16[256,16,128]{0,2,1:T(8,128)(2,1)}, u32[]{:S(2)}, u32[]{:S(2)}) async-start(bf16[256,16,128]{0,2,1:T(8,128)(2,1)} %bitcast.214), calls=%async_computation.5 | async-start | bytes 2097152 | tf_op jit(solution)/shard_map/all_to_all | solution.py:289
  160.8 29.9 %copy-start.11 = (bf16[256,2048]{1,0:T(8,128)(2,1)S(1)}, bf16[256,2048]{1,0:T(8,128)(2,1)}, u32[]{:S(2)}) copy-start(bf16[256,2048]{1,0:T(8,128)(2,1)} %get-tuple-element.243) | copy-start | bytes 3145732
  183.8 29.8 %all-to-all-start.3 = ((bf16[256,16,128]{0,2,1:T(8,128)(2,1)}), bf16[256,16,128]{0,2,1:T(8,128)(2,1)S(1)}, u32[]{:S(2)}, u32[]{:S(2)}) async-start(bf16[256,16,128]{0,2,1:T(8,128)(2,1)} %bitcast.213), calls=%async_computation.3 | async-start | bytes 2097152 | tf_op jit(solution)/shard_map/all_to_all | solution.py:288
  194.8 25.8 %copy-start.10 = (bf16[256,2048]{1,0:T(8,128)(2,1)S(1)}, bf16[256,2048]{1,0:T(8,128)(2,1)}, u32[]{:S(2)}) copy-start(bf16[256,2048]{1,0:T(8,128)(2,1)} %get-tuple-element.241) | copy-start | bytes 3145732
  213.6 11.0 %copy-start.12 = (bf16[256,16,128]{0,2,1:T(8,128)(2,1)}, bf16[256,16,128]{0,2,1:T(8,128)(2,1)S(1)}, u32[]{:S(2)}) copy-start(bf16[256,16,128]{0,2,1:T(8,128)(2,1)S(1)} %all-to-all-done.3) | copy-start | bytes 3145732
  213.6 29.9 %all-to-all-start.6 = ((bf16[256,16,128]{0,2,1:T(8,128)(2,1)}), bf16[256,16,128]{0,2,1:T(8,128)(2,1)}, u32[]{:S(2)}, u32[]{:S(2)}) async-start(bf16[256,16,128]{0,2,1:T(8,128)(2,1)} %bitcast.212), calls=%async_computation.6 | async-start | bytes 2097152 | tf_op jit(solution)/shard_map/all_to_all | solution.py:290
  243.6 83.0 %all-to-all-start.7 = ((bf16[256,16,128]{0,2,1:T(8,128)(2,1)}), bf16[256,16,128]{0,2,1:T(8,128)(2,1)}, u32[]{:S(2)}, u32[]{:S(2)}) async-start(bf16[256,16,128]{0,2,1:T(8,128)(2,1)} %bitcast.63), calls=%async_computation.7 | async-start | bytes 2097152 | tf_op jit(solution)/shard_map/all_to_all | solution.py:291
  250.5 1.6 copy-start.18
  273.2 1.6 copy-start.18
  318.6 3.0 copy-start.13
  326.5 3.0 copy-start.1
  (5 other events, 5.2 us)
where the time goes:
time: 331 us; the launch traced here: 330 us
  waiting for transfers between devices  101 us (31%)
  local copies, waits for them, and re-layouts  62.7 us (19%)
  starting transfers between devices  55.8 us (17%)
  matrix products  50.4 us (15%)
  other arithmetic  36.1 us (11%)
  blocking collectives  22 us (7%)
    dot_general x2, matrix products, filter_one_unit(): jnp.einsum('gts,tsj->jg', collected, selector, precision=lax.Precision.HI...  36.1 us
    all_gather x1, blocking collectives, body(): lax.all_gather(partial_terms * scale, 'seq', axis=1, tiled=True)  22 us
    all_to_all x1, waiting for transfers between devices, body(): lax.all_to_all(grad_query, 'seq', split_axis=1, concat_axis=0, tiled=True)  21.7 us
    all_to_all x1, waiting for transfers between devices, body(): lax.all_to_all(output_grad.T, 'seq', split_axis=0, concat_axis=1, tiled=T...  21.6 us
    all_to_all x1, waiting for transfers between devices, body(): lax.all_to_all(query_input.T, 'seq', split_axis=0, concat_axis=1, tiled=T...  20.2 us
    all_to_all x1, waiting for transfers between devices, body(): lax.all_to_all(grad_key, 'seq', split_axis=1, concat_axis=0, tiled=True)  16.6 us
    all_to_all x1, waiting for transfers between devices, body(): lax.all_to_all(section_out, 'seq', split_axis=1, concat_axis=0, tiled=True)  16.5 us
    dot_general x4, matrix products, grouped_one_unit(): jnp.einsum('kgts,gcks->gckt', masked, block_rows, preferred_element_type=...  9.15 us
  transfers between devices with their start and end apart: 8, of which 7 were waited for; matrix products, arithmetic and copies ran while one was open for 33% of the time, Pallas kernels for 0%

commit v1 on v0

v1 whole, which is shorter than its diff:
```python
import functools
import math

import jax
import jax.numpy as jnp
from jax import lax
from jax.experimental import pallas as pl
from jax.experimental.pallas import tpu as pltpu
from jax.sharding import PartitionSpec as P

MESH = pl.DeviceIdType.MESH
LANES = 128
RB = 16
PAD = 16


def lanes_of(index):
    return pl.ds(pl.multiple_of(index * LANES, LANES), LANES)


def kernel(
    n, chunks, width,
    q_ref, k_ref, v_ref, d_ref, taps_ref, base_ref, gain_ref, mshort_ref, mf_ref, mb_ref, lm_ref,
    so_ref, gq_ref, gk_ref, gv_ref, f_ref,
    rim_q, rim_k, rim_v, xf, xb, qs, ks, vs, hf, hb, eq, ek, ev, scr,
    rim_ss, rim_rs, gp_ss, gp_rs, cg_ss, cg_rs, eb_ss, eb_rs,
):
    rows, channels = q_ref.shape
    short = taps_ref.shape[1]
    groups = LANES // width
    steps = channels // LANES // chunks
    me = lax.axis_index("seq")
    grp = lax.axis_index("grp")
    has_left = me > 0
    has_right = me < n - 1
    left = (grp, lax.max(me - 1, 0))
    right = (grp, lax.min(me + 1, n - 1))
    f32, bf16 = jnp.float32, jnp.bfloat16
    barrier = pltpu.get_barrier_semaphore()

    @pl.when(has_left)
    def _():
        pl.semaphore_signal(barrier, inc=1, device_id=left, device_id_type=MESH)

    @pl.when(has_right)
    def _():
        pl.semaphore_signal(barrier, inc=1, device_id=right, device_id_type=MESH)

    pl.semaphore_wait(barrier, jnp.where(has_left, 1, 0) + jnp.where(has_right, 1, 0))

    def remote(src, dst, ssem, rsem, where):
        return pltpu.make_async_remote_copy(
            src_ref=src, dst_ref=dst, send_sem=ssem, recv_sem=rsem, device_id=where, device_id_type=MESH
        )

    rim_copies = [
        remote(src.at[pl.ds(rows - PAD, PAD), :], dst, rim_ss.at[i], rim_rs.at[i], right)
        for i, (src, dst) in enumerate(((q_ref, rim_q), (k_ref, rim_k), (v_ref, rim_v)))
    ]

    @pl.when(has_right)
    def _():
        for copy in rim_copies:
            copy.start()

    taps = rows
    window = 2 * taps
    rest = xf.shape[0] - 2 * rows
    xf[pl.ds(2 * rows, rest), :] = jnp.zeros((rest, channels), bf16)
    xb[pl.ds(2 * rows, rest), :] = jnp.zeros((rest, channels), bf16)

    def build(i, carry):
        for which, dest in ((0, hf), (1, hb)):
            tile = base_ref[which, pl.ds(pl.multiple_of(i * groups, groups), groups), :]
            for g in range(groups):
                row = jnp.broadcast_to(tile[g : g + 1, :], (RB, window))
                skew = pltpu.roll(row, 0, 1, stride=1, stride_axis=0)
                dest[pl.ds(pl.multiple_of((i * groups + g) * RB, RB), RB), :] = skew.astype(bf16)
        return carry

    lax.fori_loop(0, channels // LANES, build, 0)

    @pl.when(has_left)
    def _():
        for copy in rim_copies:
            copy.wait_recv()

    @pl.when(jnp.logical_not(has_left))
    def _():
        for rim in (rim_q, rim_k, rim_v):
            rim[...] = jnp.zeros_like(rim)
        xf[pl.ds(0, rows), :] = jnp.zeros((rows, channels), bf16)

    @pl.when(jnp.logical_not(has_right))
    def _():
        xb[pl.ds(rows, rows), :] = jnp.zeros((rows, channels), bf16)
        for rim in (eq, ek, ev):
            rim[pl.ds(rows, PAD), :] = jnp.zeros((PAD, channels), bf16)

    def forward(slot, x_ref, rim, col):
        scr[slot, 0:PAD, :] = rim[:, col].astype(f32)
        scr[slot, PAD : PAD + rows, :] = x_ref[:, col].astype(f32)
        total = taps_ref[slot, 0:1, col] * scr[slot, PAD : PAD + rows, :]
        for j in range(1, short):
            total = total + taps_ref[slot, j : j + 1, col] * (
                mshort_ref[j - 1] * scr[slot, PAD - j : PAD - j + rows, :]
            )
        return total

    def first(i, carry):
        col = lanes_of(i)
        query = forward(0, q_ref, rim_q, col)
        qs[:, col] = query
        xb[0:rows, col] = (d_ref[:, col].astype(f32) * query).astype(bf16)
        key = forward(1, k_ref, rim_k, col)
        ks[:, col] = key
        value = forward(2, v_ref, rim_v, col)
        vs[:, col] = value
        xf[rows : 2 * rows, col] = (key * value).astype(bf16)
        return carry

    gp_copies, cg_copies, eb_copies = [], [], []
    for chunk in range(chunks):
        lo = chunk * steps * LANES
        span = pl.ds(lo, steps * LANES)
        gp_copies.append(remote(
            xf.at[pl.ds(rows, rows), span], xf.at[pl.ds(0, rows), span], gp_ss.at[chunk], gp_rs.at[chunk], right))
        cg_copies.append(remote(
            xb.at[pl.ds(0, rows), span], xb.at[pl.ds(rows, rows), span], cg_ss.at[chunk], cg_rs.at[chunk], left))
        eb_copies.append([
            remote(e.at[pl.ds(0, PAD), span], e.at[pl.ds(rows, PAD), span],
                   eb_ss.at[chunk * 3 + i], eb_rs.at[chunk * 3 + i], left)
            for i, e in enumerate((eq, ek, ev))
        ])

    for chunk in range(chunks):
        lax.fori_loop(chunk * steps, (chunk + 1) * steps, first, 0)

        @pl.when(has_right)
        def _():
            gp_copies[chunk].start()

        @pl.when(has_left)
        def _():
            cg_copies[chunk].start()

    lane_group = lax.broadcasted_iota(jnp.int32, (RB, LANES), 1) // width

    def diagonal(out):
        y = out[0:RB]
        for g in range(1, groups):
            y = jnp.where(lane_group == g, out[g * RB : (g + 1) * RB], y)
        return y

    def second(i, carry):
        col = lanes_of(i)
        hrows = pl.ds(pl.multiple_of(i * groups * RB, groups * RB), groups * RB)
        gain = gain_ref[0:1, col]
        total = None
        for a in range(rows // RB):
            own = slice(a * RB, (a + 1) * RB)
            mf = mf_ref[own, :]
            source = xf[a * RB : a * RB + window, col]
            grads = xb[a * RB : a * RB + window, col]
            table = (hf[hrows, :].reshape(groups, RB, window) * mf[None]).reshape(groups * RB, window)
            conv = diagonal(jnp.dot(table, source, preferred_element_type=f32))
            pair = xf[rows + a * RB : rows + (a + 1) * RB, col]
            conv = conv + gain * pair.astype(f32)
            so_ref[own, col] = (qs[own, col] * conv).astype(bf16)
            eq[own, col] = (d_ref[own, col].astype(f32) * conv).astype(bf16)
            table = (hb[hrows, :].reshape(groups, RB, window) * mb_ref[own, :][None]).reshape(groups * RB, window)
            back = diagonal(jnp.dot(table, grads, preferred_element_type=f32))
            grad = xb[own, col]
            back = back + gain * grad.astype(f32)
            ek[own, col] = (back * vs[own, col]).astype(bf16)
            ev[own, col] = (back * ks[own, col]).astype(bf16)
            spread = (grad[None] * lm_ref[...]).reshape(groups * RB, LANES)
            terms = lax.dot_general(spread, source, (((1,), (1,)), ((), ())), preferred_element_type=f32)
            terms = terms.reshape(groups, RB, window) * mf.astype(f32)[None]
            total = terms if total is None else total + terms
        half = RB // 2
        upper = total[:, half:].reshape(groups * half, window)
        total = total[:, :half].reshape(groups * half, window) + pltpu.roll(upper, window - half, 1)
        sub = lax.broadcasted_iota(jnp.int32, (groups * half, window), 0)
        shift = 1
        while shift < half:
            total = jnp.where((sub & shift) != 0, pltpu.roll(total, window - shift, 1), total)
            shift *= 2
        terms = jnp.sum(total.reshape(groups, half, window), axis=1)
        terms = pltpu.roll(terms, window - 1, 1)
        f_ref[pl.ds(pl.multiple_of(i * groups, groups), groups), :] = terms[:, :taps]
        return carry

    for chunk in range(chunks):
        @pl.when(has_left)
        def _():
            gp_copies[chunk].wait_recv()

        @pl.when(has_right)
        def _():
            cg_copies[chunk].wait_recv()

        lax.fori_loop(chunk * steps, (chunk + 1) * steps, second, 0)

        @pl.when(has_left)
        def _():
            for copy in eb_copies[chunk]:
                copy.start()

    def backward(slot, e_ref, out_ref, col):
        scr[slot] = e_ref[:, col].astype(f32)
        total = taps_ref[slot, 0:1, col] * scr[slot, 0:rows, :]
        for j in range(1, short):
            total = total + taps_ref[slot, j : j + 1, col] * (
                mshort_ref[short - 2 + j] * scr[slot, j : j + rows, :]
            )
        out_ref[:, col] = total.astype(bf16)

    def third(i, carry):
        col = lanes_of(i)
        backward(0, eq, gq_ref, col)
        backward(1, ek, gk_ref, col)
        backward(2, ev, gv_ref, col)
        return carry

    for chunk in range(chunks):
        @pl.when(has_right)
        def _():
            for copy in eb_copies[chunk]:
                copy.wait_recv()

        lax.fori_loop(chunk * steps, (chunk + 1) * steps, third, 0)

    @pl.when(has_right)
    def _():
        for copy in rim_copies:
            copy.wait_send()
        for copy in gp_copies:
            copy.wait_send()

    @pl.when(has_left)
    def _():
        for copy in cg_copies:
            copy.wait_send()
        for copies in eb_copies:
            for copy in copies:
                copy.wait_send()


def body(q, k, v, d, short_taps, long_filter, skip_gain, genome_ids):
    rows, channels = q.shape
    taps, filters = long_filter.shape
    width = channels // filters
    groups = LANES // width
    short = short_taps.shape[1]
    n = lax.axis_size("seq")
    me = lax.axis_index("seq")
    f32, bf16 = jnp.float32, jnp.bfloat16
    window = 2 * taps
    chunks = 4
    ext = 2 * rows + window - RB - rows
    ext = max(ext, 3 * rows - RB)

    padded = jnp.pad(genome_ids, (taps, 2 * taps), constant_values=-1)
    ids = lax.dynamic_slice_in_dim(padded, me * rows, 2 * taps + 2 * rows, 0)
    own = ids[taps : taps + rows]
    blocks = rows // RB
    front = jnp.stack([ids[a * RB : a * RB + window] for a in range(blocks)])
    back = jnp.stack([ids[taps + a * RB : taps + a * RB + window] for a in range(blocks)])
    own_blocks = own.reshape(blocks, RB, 1)
    mf = (own_blocks == front[:, None, :]).astype(bf16).reshape(rows, window)
    mb = (own_blocks == back[:, None, :]).astype(bf16).reshape(rows, window)
    mshort = jnp.stack(
        [own == ids[taps - j : taps - j + rows] for j in range(1, short)]
        + [own == ids[taps + j : taps + j + rows] for j in range(1, short)]
    ).astype(f32)
    mshort = jnp.broadcast_to(mshort[:, :, None], (2 * (short - 1), rows, LANES))
    filt = long_filter.astype(f32).T
    base = jnp.stack([
        jnp.pad(filt[:, ::-1], ((0, 0), (1, window - taps - 1))),
        jnp.pad(filt, ((0, 0), (0, window - taps))),
    ])
    lane = lax.broadcasted_iota(jnp.int32, (groups, RB, LANES), 2) // width
    lm = (lane == lax.broadcasted_iota(jnp.int32, (groups, RB, LANES), 0)).astype(bf16)

    big = jax.ShapeDtypeStruct((rows, channels), bf16)
    vm = pl.BlockSpec(memory_space=pltpu.VMEM)
    dma = pltpu.SemaphoreType.DMA
    so, gq, gk, gv, terms = pl.pallas_call(
        functools.partial(kernel, n, chunks, width),
        out_shape=(big, big, big, big, jax.ShapeDtypeStruct((filters, taps), f32)),
        in_specs=[vm] * 11,
        out_specs=(vm,) * 5,
        scratch_shapes=[
            pltpu.VMEM((PAD, channels), bf16),
            pltpu.VMEM((PAD, channels), bf16),
            pltpu.VMEM((PAD, channels), bf16),
            pltpu.VMEM((ext, channels), bf16),
            pltpu.VMEM((ext, channels), bf16),
            pltpu.VMEM((rows, channels), f32),
            pltpu.VMEM((rows, channels), f32),
            pltpu.VMEM((rows, channels), f32),
            pltpu.VMEM((filters * RB, window), bf16),
            pltpu.VMEM((filters * RB, window), bf16),
            pltpu.VMEM((rows + PAD, channels), bf16),
            pltpu.VMEM((rows + PAD, channels), bf16),
            pltpu.VMEM((rows + PAD, channels), bf16),
            pltpu.VMEM((3, rows + PAD, LANES), f32),
            dma((3,)), dma((3,)),
            dma((chunks,)), dma((chunks,)),
            dma((chunks,)), dma((chunks,)),
            dma((3 * chunks,)), dma((3 * chunks,)),
        ],
        compiler_params=pltpu.CompilerParams(
            collective_id=0, has_side_effects=True, vmem_limit_bytes=56 * 1024 * 1024
        ),
    )(q, k, v, d, short_taps, base, skip_gain.reshape(1, channels), mshort, mf, mb, lm)
    scale = 1.0 / math.sqrt(width * rows * n)
    summed = lax.psum(terms, "seq")
    return so, gq, gk, gv, summed[:, ::-1].T * scale


def solution(mesh):
    tile = P(("grp", "seq"), None)
    return jax.shard_map(
        body,
        mesh=mesh,
        in_specs=(tile, tile, tile, tile, P(), P(), P(), P("grp")),
        out_specs=(tile, tile, tile, tile, P("grp", None)),
        check_vma=False,
    )
```

time: 331 us -> 184 us (0.56)
  starting transfers between devices: 55.8 us -> 0.04 us
  Pallas kernels: 0 us -> 53.9 us
  local copies, waits for them, and re-layouts: 62.7 us -> 11.5 us
  matrix products: 50.4 us -> 0 us
  other arithmetic: 36.1 us -> 3.3 us
  blocking collectives: 22 us -> 0 us
  between operations: 1.12 us -> 14.1 us
    all_to_all x8 -> x0, waiting for transfers between devices: 101 us -> none  [the longest x1 21.7 us: body(): lax.all_to_all(grad_query, 'seq', split_axis=1, concat_axis=0, tiled=True)]
    psum x0 -> x1, waiting for transfers between devices: none -> 99.5 us  [body(): summed = lax.psum(terms, 'seq')]
    all_to_all x8 -> x0, starting transfers between devices: 55.8 us -> none  [the longest x1 7.36 us: body(): lax.all_to_all(output_grad.T, 'seq', split_axis=0, concat_axis=1, tiled=T...]
    pallas_call x0 -> x1, Pallas kernels: none -> 53.9 us  [body(): pl.pallas_call(functools.partial(kernel, n, chunks, width), out_shape=(bi...]
    dot_general x8 -> x0, matrix products: 50.4 us -> none  [the longest x2 36.1 us: filter_one_unit(): jnp.einsum('gts,tsj->jg', collected, selector, precision=lax.Precision.HI...]
    convert_element_type x14 -> x3, other arithmetic: 34.3 us -> 1.37 us  [the longest x1 0.74 us: body(): mb = (own_blocks == back[:, None, :]).astype(bf16).reshape(rows, window)]
    all_gather x1 -> x0, blocking collectives: 22 us -> none  [body(): lax.all_gather(partial_terms * scale, 'seq', axis=1, tiled=True)]
    another operation x6 -> x4, local copies, waits for them, and re-layouts: 12.1 us -> 0.26 us  [the longest x1 0.14 us: body(): jnp.stack([jnp.pad(filt[:, ::-1], ((0, 0), (1, window - taps - 1))), jnp....]
  transfers between devices with their start and end apart: 8 -> 1, of which waited for: 7 -> 1; matrix products, arithmetic and copies ran while one was open for 33% -> 0% of each run, Pallas kernels for 0% -> 0%
where the time goes in v1:
time: 184 us; the launch traced here: 182 us
  waiting for transfers between devices  99.5 us (54%)
  Pallas kernels  53.9 us (29%)
  between operations  14.1 us (8%)
  local copies, waits for them, and re-layouts  11.5 us (6%)
  other arithmetic  3.3 us (2%)
    psum x1, waiting for transfers between devices, body(): summed = lax.psum(terms, 'seq')  99.5 us
    pallas_call x1, Pallas kernels, body(): pl.pallas_call(functools.partial(kernel, n, chunks, width), out_shape=(bi...  53.9 us
    unnamed x14, local copies, waits for them, and re-layouts  7.42 us
  transfers between devices with their start and end apart: 1, of which 1 were waited for; matrix products, arithmetic and copies ran while one was open for 0% of the time, Pallas kernels for 0%

profile of v1, /device:TPU:0, one launch (start us, length us, event | category | flops | bytes accessed | tf_op | source)
XLA Modules:
  0.0 182.4 jit_solution(15818227202413940582)
XLA Ops:
  7.2 0.0 copy-start.3
  7.2 0.0 all-reduce.5.cloned.1.call-start
  7.3 0.8 pad_dynamic-slice_fusion
  8.0 0.1 compare_bitcast_fusion.9
  8.1 0.1 compare_bitcast_fusion
  8.2 0.1 fusion.3
  8.3 0.1 stack.117
  8.4 0.0 copy-done.3
  8.4 0.1 copy.13
  8.5 0.2 rev.6
  8.7 0.1 pad_bitcast_fusion
  8.8 0.8 pad_maximum_fusion.base_ref
  9.7 0.6 fusion.2.lm_ref
  10.4 0.7 fusion.1
  11.1 1.1 broadcast_in_dim.2.mshort_ref
  12.2 53.9 %shard_map.119 = (bf16[128,4096]{1,0:T(8,128)(2,1)}, bf16[128,4096]{1,0:T(8,128)(2,1)}, bf16[128,4096]{1,0:T(8,128)(2,1)}, bf16[128,4096]{1,0:T(8,128)(2,1)}, f32[256,128]{1,0:T(8,128)}) custom-call(bf16[128,4096]{1,0:T(8,128)(2,1)} %q_ref.1, bf16[128,4096]{1,0:T(8,128)(2,1)} %k_ref.1, bf16[128,4096]{1,0:T(8,128)(2,1)} %v_ref.1, bf16[128,4096]{1,0:T(8,128)(2,1)} %d_ref.1, ...), custom_call_target="tpu_custom_call" | custom-call | tf_op jit(solution)/shard_map/pallas_call | solution.py:289
  66.2 1.6 rev.7
  67.8 0.0 all-reduce.5.cloned.1.call-update
  67.8 99.5 %all-reduce.5.cloned.1.call-done = f32[256,128]{1,0:T(8,128)} async-done(((f32[256,128]{1,0:T(8,128)}), f32[256,128]{1,0:T(8,128)}) %all-reduce.5.cloned.1.call-update) | async-done | bytes 131088 | tf_op jit(solution)/shard_map/psum | solution.py:319
  167.3 0.9 multiply_bitcast_fusion
  168.2 0.8 copy.14
  169.0 0.0 copy-start.2
  169.0 2.4 %copy.20 = bf16[128,4096]{1,0:T(8,128)(2,1)} copy(bf16[128,4096]{1,0:T(8,128)(2,1)} %get-tuple-element.59) | data formatting | bytes 2097152
  171.3 0.0 copy-done.2
  171.3 0.0 copy-start.1
  171.3 1.0 copy.21
  172.3 0.6 copy-done.1
  172.9 0.0 copy-start
  172.9 1.0 copy.22
  173.9 0.6 copy-done
  174.6 1.0 copy.23
  (7 shorter events, 0.1 us)
Async XLA Ops:
  7.2 1.2 copy-start.3
  7.2 160.1 %all-reduce.5.cloned.1.call-start = ((), (), s32[]{:S(2)}) async-start(), calls=%async_computation | async-start | bytes 262144 | tf_op jit(solution)/shard_map/psum | solution.py:319
  169.0 2.4 %copy-start.2 = (bf16[128,4096]{1,0:T(8,128)(2,1)S(1)}, bf16[128,4096]{1,0:T(8,128)(2,1)}, u32[]{:S(2)}) copy-start(bf16[128,4096]{1,0:T(8,128)(2,1)} %get-tuple-element.60) | copy-start | bytes 3145732
  171.3 1.6 copy-start.1
  172.9 1.6 copy-start
Sparse Core Ops, SparseCore 0:
  68.0 99.2 all-reduce.4

commit v2 on v1

--- a/solution.py
+++ b/solution.py
@@ -12,6 +12,7 @@
 LANES = 128
 RB = 16
 PAD = 16
+DEPTH = 3
 
 
 def lanes_of(index):
@@ -19,11 +20,11 @@
 
 
 def kernel(
-    n, chunks, width,
-    q_ref, k_ref, v_ref, d_ref, taps_ref, base_ref, gain_ref, mshort_ref, mf_ref, mb_ref, lm_ref,
+    n, chunks, width, scale,
+    q_ref, k_ref, v_ref, d_ref, taps_ref, base_ref, gain_ref, mshort_ref, mf_ref, mb_ref, lm_ref, mt_ref,
     so_ref, gq_ref, gk_ref, gv_ref, f_ref,
     rim_q, rim_k, rim_v, xf, xb, qs, ks, vs, hf, hb, eq, ek, ev, scr,
-    rim_ss, rim_rs, gp_ss, gp_rs, cg_ss, cg_rs, eb_ss, eb_rs,
+    parts, inbox, done, rim_ss, rim_rs, gp_ss, gp_rs, cg_ss, cg_rs, eb_ss, eb_rs, ps_ss, ps_rs, bc_ss, bc_rs,
 ):
     rows, channels = q_ref.shape
     short = taps_ref.shape[1]
@@ -38,15 +39,15 @@
     f32, bf16 = jnp.float32, jnp.bfloat16
     barrier = pltpu.get_barrier_semaphore()
 
-    @pl.when(has_left)
-    def _():
-        pl.semaphore_signal(barrier, inc=1, device_id=left, device_id_type=MESH)
-
-    @pl.when(has_right)
-    def _():
-        pl.semaphore_signal(barrier, inc=1, device_id=right, device_id_type=MESH)
-
-    pl.semaphore_wait(barrier, jnp.where(has_left, 1, 0) + jnp.where(has_right, 1, 0))
+    def peer_of(offset):
+        return lax.rem(me + offset, n)
+
+    def greet(offset, carry):
+        pl.semaphore_signal(barrier, inc=1, device_id=(grp, peer_of(offset)), device_id_type=MESH)
+        return carry
+
+    lax.fori_loop(1, n, greet, 0)
+    pl.semaphore_wait(barrier, n - 1)
 
     def remote(src, dst, ssem, rsem, where):
         return pltpu.make_async_remote_copy(
@@ -65,6 +66,7 @@
 
     taps = rows
     window = 2 * taps
+    reach = taps + RB
     rest = xf.shape[0] - 2 * rows
     xf[pl.ds(2 * rows, rest), :] = jnp.zeros((rest, channels), bf16)
     xb[pl.ds(2 * rows, rest), :] = jnp.zeros((rest, channels), bf16)
@@ -136,13 +138,14 @@
     for chunk in range(chunks):
         lax.fori_loop(chunk * steps, (chunk + 1) * steps, first, 0)
 
-        @pl.when(has_right)
-        def _():
-            gp_copies[chunk].start()
-
-        @pl.when(has_left)
-        def _():
-            cg_copies[chunk].start()
+        if chunk < DEPTH:
+            @pl.when(has_right)
+            def _():
+                gp_copies[chunk].start()
+
+            @pl.when(has_left)
+            def _():
+                cg_copies[chunk].start()
 
     lane_group = lax.broadcasted_iota(jnp.int32, (RB, LANES), 1) // width
 
@@ -151,6 +154,21 @@
         for g in range(1, groups):
             y = jnp.where(lane_group == g, out[g * RB : (g + 1) * RB], y)
         return y
+
+    def part_copy(owner, sender):
+        return remote(parts.at[owner], inbox.at[sender], ps_ss.at[owner], ps_rs.at[sender], (grp, owner))
+
+    def done_copy(owner, peer):
+        return remote(done.at[owner], done.at[owner], bc_ss.at[peer], bc_rs.at[owner], (grp, peer))
+
+    def over_peers(act):
+        def step(offset, carry):
+            act(peer_of(offset))
+            return carry
+
+        lax.fori_loop(1, n, step, 0)
+
+    per = parts.shape[1]
 
     def second(i, carry):
         col = lanes_of(i)
@@ -175,9 +193,12 @@
             ek[own, col] = (back * vs[own, col]).astype(bf16)
             ev[own, col] = (back * ks[own, col]).astype(bf16)
             spread = (grad[None] * lm_ref[...]).reshape(groups * RB, LANES)
-            terms = lax.dot_general(spread, source, (((1,), (1,)), ((), ())), preferred_element_type=f32)
-            terms = terms.reshape(groups, RB, window) * mf.astype(f32)[None]
+            terms = lax.dot_general(
+                xf[a * RB : a * RB + reach, col], spread, (((1,), (1,)), ((), ())), preferred_element_type=f32)
+            terms = terms * mt_ref[a]
             total = terms if total is None else total + terms
+        total = jnp.concatenate([total, jnp.zeros((window - reach, groups * RB), f32)], axis=0)
+        total = total.T.reshape(groups, RB, window)
         half = RB // 2
         upper = total[:, half:].reshape(groups * half, window)
         total = total[:, :half].reshape(groups * half, window) + pltpu.roll(upper, window - half, 1)
@@ -188,7 +209,11 @@
             shift *= 2
         terms = jnp.sum(total.reshape(groups, half, window), axis=1)
         terms = pltpu.roll(terms, window - 1, 1)
-        f_ref[pl.ds(pl.multiple_of(i * groups, groups), groups), :] = terms[:, :taps]
+        if per >= groups:
+            parts[i * groups // per, pl.ds(pl.multiple_of(i * groups % per, groups), groups), :] = terms[:, :taps]
+        else:
+            for m in range(groups // per):
+                parts[i * (groups // per) + m] = terms[m * per : (m + 1) * per, :taps]
         return carry
 
     for chunk in range(chunks):
@@ -200,12 +225,25 @@
         def _():
             cg_copies[chunk].wait_recv()
 
+        if chunk + DEPTH < chunks:
+            @pl.when(has_right)
+            def _():
+                gp_copies[chunk].wait_send()
+                gp_copies[chunk + DEPTH].start()
+
+            @pl.when(has_left)
+            def _():
+                cg_copies[chunk].wait_send()
+                cg_copies[chunk + DEPTH].start()
+
         lax.fori_loop(chunk * steps, (chunk + 1) * steps, second, 0)
 
         @pl.when(has_left)
         def _():
             for copy in eb_copies[chunk]:
                 copy.start()
+
+    over_peers(lambda peer: part_copy(peer, me).start())
 
     def backward(slot, e_ref, out_ref, col):
         scr[slot] = e_ref[:, col].astype(f32)
@@ -230,21 +268,41 @@
                 copy.wait_recv()
 
         lax.fori_loop(chunk * steps, (chunk + 1) * steps, third, 0)
+        if chunk == chunks // 2 - 1:
+            over_peers(lambda peer: part_copy(peer, peer).wait_recv())
+            total = parts[me]
+
+            def add(offset, total):
+                return total + inbox[peer_of(offset)]
+
+            done[me] = lax.fori_loop(1, n, add, total)
+            over_peers(lambda peer: done_copy(me, peer).start())
 
     @pl.when(has_right)
     def _():
         for copy in rim_copies:
             copy.wait_send()
-        for copy in gp_copies:
+        for copy in gp_copies[chunks - DEPTH :]:
             copy.wait_send()
 
     @pl.when(has_left)
     def _():
-        for copy in cg_copies:
+        for copy in cg_copies[chunks - DEPTH :]:
             copy.wait_send()
         for copies in eb_copies:
             for copy in copies:
                 copy.wait_send()
+
+    over_peers(lambda peer: part_copy(peer, peer).wait_send())
+    over_peers(lambda peer: done_copy(peer, peer).wait_recv())
+    over_peers(lambda peer: done_copy(me, peer).wait_send())
+    flip = (
+        lax.broadcasted_iota(jnp.int32, (taps, taps), 0) + lax.broadcasted_iota(jnp.int32, (taps, taps), 1)
+        == taps - 1
+    ).astype(f32)
+    f_ref[...] = scale * lax.dot_general(
+        flip, done[...].reshape(n * per, taps), (((1,), (1,)), ((), ())),
+        precision=lax.Precision.HIGHEST, preferred_element_type=f32)
 
 
 def body(q, k, v, d, short_taps, long_filter, skip_gain, genome_ids):
@@ -257,7 +315,7 @@
     me = lax.axis_index("seq")
     f32, bf16 = jnp.float32, jnp.bfloat16
     window = 2 * taps
-    chunks = 4
+    chunks = 8
     ext = 2 * rows + window - RB - rows
     ext = max(ext, 3 * rows - RB)
 
@@ -270,6 +328,8 @@
     own_blocks = own.reshape(blocks, RB, 1)
     mf = (own_blocks == front[:, None, :]).astype(bf16).reshape(rows, window)
     mb = (own_blocks == back[:, None, :]).astype(bf16).reshape(rows, window)
+    same_t = (own.reshape(blocks, 1, RB) == front[:, : taps + RB, None]).astype(f32)
+    mt = jnp.tile(same_t, (1, 1, groups))
     mshort = jnp.stack(
         [own == ids[taps - j : taps - j + rows] for j in range(1, short)]
         + [own == ids[taps + j : taps + j + rows] for j in range(1, short)]
@@ -283,13 +343,14 @@
     lane = lax.broadcasted_iota(jnp.int32, (groups, RB, LANES), 2) // width
     lm = (lane == lax.broadcasted_iota(jnp.int32, (groups, RB, LANES), 0)).astype(bf16)
 
+    scale = 1.0 / math.sqrt(width * rows * n)
     big = jax.ShapeDtypeStruct((rows, channels), bf16)
     vm = pl.BlockSpec(memory_space=pltpu.VMEM)
     dma = pltpu.SemaphoreType.DMA
     so, gq, gk, gv, terms = pl.pallas_call(
-        functools.partial(kernel, n, chunks, width),
-        out_shape=(big, big, big, big, jax.ShapeDtypeStruct((filters, taps), f32)),
-        in_specs=[vm] * 11,
+        functools.partial(kernel, n, chunks, width, scale),
+        out_shape=(big, big, big, big, jax.ShapeDtypeStruct((taps, filters), f32)),
+        in_specs=[vm] * 12,
         out_specs=(vm,) * 5,
         scratch_shapes=[
             pltpu.VMEM((PAD, channels), bf16),
@@ -306,18 +367,20 @@
             pltpu.VMEM((rows + PAD, channels), bf16),
             pltpu.VMEM((rows + PAD, channels), bf16),
             pltpu.VMEM((3, rows + PAD, LANES), f32),
+            pltpu.VMEM((n, filters // n, taps), f32),
+            pltpu.VMEM((n, filters // n, taps), f32),
+            pltpu.VMEM((n, filters // n, taps), f32),
             dma((3,)), dma((3,)),
             dma((chunks,)), dma((chunks,)),
             dma((chunks,)), dma((chunks,)),
             dma((3 * chunks,)), dma((3 * chunks,)),
+            dma((n,)), dma((n,)), dma((n,)), dma((n,)),
         ],
         compiler_params=pltpu.CompilerParams(
             collective_id=0, has_side_effects=True, vmem_limit_bytes=56 * 1024 * 1024
         ),
-    )(q, k, v, d, short_taps, base, skip_gain.reshape(1, channels), mshort, mf, mb, lm)
-    scale = 1.0 / math.sqrt(width * rows * n)
-    summed = lax.psum(terms, "seq")
-    return so, gq, gk, gv, summed[:, ::-1].T * scale
+    )(q, k, v, d, short_taps, base, skip_gain.reshape(1, channels), mshort, mf, mb, lm, mt)
+    return so, gq, gk, gv, terms
 
 
 def solution(mesh):

time: 184 us -> 83.4 us (0.45)
  waiting for transfers between devices: 99.5 us -> 0 us
  Pallas kernels: 53.9 us -> 68.5 us
  between operations: 14.1 us -> 0.73 us
    psum x1 -> x0, waiting for transfers between devices: 99.5 us -> none  [body(): summed = lax.psum(terms, 'seq')]
    pallas_call x1, Pallas kernels: 53.9 us -> 68.5 us  [body(): pl.pallas_call(functools.partial(kernel, n, chunks, width, scale), out_sh...]
    unnamed x14 -> x18, local copies, waits for them, and re-layouts: 7.42 us -> 8.2 us
  transfers between devices with their start and end apart: 1 -> 0, of which waited for: 1 -> 0; matrix products, arithmetic and copies ran while one was open for 0% -> 0% of each run, Pallas kernels for 0% -> 0%
where the time goes in v2:
time: 83.4 us; the launch traced here: 83 us
  Pallas kernels  68.5 us (82%)
  local copies, waits for them, and re-layouts  11.3 us (14%)
  other arithmetic  2.47 us (3%)
    pallas_call x1, Pallas kernels, body(): pl.pallas_call(functools.partial(kernel, n, chunks, width, scale), out_sh...  68.5 us
    unnamed x18, local copies, waits for them, and re-layouts  8.2 us

profile of v2, /device:TPU:0, one launch (start us, length us, event | category | flops | bytes accessed | tf_op | source)
XLA Modules:
  0.0 83.0 jit_solution(10536265576246852318)
XLA Ops:
  0.6 0.0 copy-start.5
  0.7 0.7 copy-done.5
  1.3 0.1 pad_dynamic-slice_fusion
  1.4 0.1 compare_bitcast_fusion.9
  1.5 0.1 eq.108
  1.6 0.1 compare_bitcast_fusion
  1.7 0.1 stack.117
  1.7 0.1 fusion.3
  1.8 0.0 copy-start.4
  1.9 0.6 fusion.2.lm_ref
  2.5 0.2 copy-done.4
  2.7 0.1 copy.14
  2.8 0.7 fusion.1
  3.5 0.1 compare_convert_fusion
  3.6 0.2 rev.3
  3.8 0.1 pad_bitcast_fusion
  4.0 0.8 %pad_maximum_fusion.base_ref = f32[2,256,256]{2,1,0:T(8,128)} fusion(f32[1,256,256]{2,1,0:T(8,128)S(1)} %get-tuple-element.35, f32[1,256,256]{2,1,0:T(8,128)S(1)} %get-tuple-element.36), kind=kLoop, calls=%fused_computation | loop fusion | flops 131072 | bytes 1048576 | tf_op jit(solution)/shard_map/stack | solution.py:339
  4.8 1.1 %broadcast_in_dim.2.mshort_ref = f32[12,128,128]{2,1,0:T(8,128)} broadcast(f32[12,128]{1,0:T(8,128)S(1)} %convert_element_type.30), dimensions={0,1} | broadcast | bytes 792576 | tf_op jit(solution)/shard_map/broadcast_in_dim | solution.py:337
  5.9 0.1 tile.4
  6.1 1.2 %copy.15.mt_ref = f32[8,144,128]{2,1,0:T(8,128)} copy(f32[8,144,128]{1,2,0:T(8,128)S(1)} %bitcast.57) | data formatting | bytes 1179648 | tf_op jit(solution)/shard_map/tile | solution.py:332
  7.2 68.5 %shard_map.119 = (bf16[128,4096]{1,0:T(8,128)(2,1)}, bf16[128,4096]{1,0:T(8,128)(2,1)}, bf16[128,4096]{1,0:T(8,128)(2,1)}, bf16[128,4096]{1,0:T(8,128)(2,1)}, f32[128,256]{1,0:T(8,128)}) custom-call(bf16[128,4096]{1,0:T(8,128)(2,1)} %q_ref.1, bf16[128,4096]{1,0:T(8,128)(2,1)} %k_ref.1, bf16[128,4096]{1,0:T(8,128)(2,1)} %v_ref.1, bf16[128,4096]{1,0:T(8,128)(2,1)} %d_ref.1, ...), custom_call_target="tpu_custom_call" | custom-call | tf_op jit(solution)/shard_map/pallas_call | solution.py:350
  75.8 0.0 copy-start.2
  75.8 2.4 %copy.21 = bf16[128,4096]{1,0:T(8,128)(2,1)} copy(bf16[128,4096]{1,0:T(8,128)(2,1)} %get-tuple-element.44) | data formatting | bytes 2097152
  78.2 0.0 copy-done.2
  78.2 0.0 copy-start.1
  78.2 1.0 %copy.22 = bf16[128,4096]{1,0:T(8,128)(2,1)} copy(bf16[128,4096]{1,0:T(8,128)(2,1)S(1)} %copy-done.2) | data formatting | bytes 2097152
  79.1 0.6 copy-done.1
  79.8 1.0 %copy.23 = bf16[128,4096]{1,0:T(8,128)(2,1)} copy(bf16[128,4096]{1,0:T(8,128)(2,1)S(1)} %copy-done.1) | data formatting | bytes 2097152
  80.7 0.6 copy-done
  81.4 1.0 %copy.24 = bf16[128,4096]{1,0:T(8,128)(2,1)} copy(bf16[128,4096]{1,0:T(8,128)(2,1)S(1)} %copy-done) | data formatting | bytes 2097152
  82.3 0.1 copy-done.3
  82.4 0.7 copy.25
  (9 shorter events, 0.1 us)
Async XLA Ops:
  0.6 0.7 copy-start.5
  1.8 0.8 %copy-start.4 = (bf16[128,256]{1,0:T(8,128)(2,1)S(1)}, bf16[128,256]{1,0:T(8,128)(2,1)}, u32[]{:S(2)}) copy-start(bf16[128,256]{1,0:T(8,128)(2,1)} %param.13) | copy-start | bytes 196612
  75.8 2.4 %copy-start.2 = (bf16[128,4096]{1,0:T(8,128)(2,1)S(1)}, bf16[128,4096]{1,0:T(8,128)(2,1)}, u32[]{:S(2)}) copy-start(bf16[128,4096]{1,0:T(8,128)(2,1)} %get-tuple-element.45) | copy-start | bytes 3145732
  78.2 1.6 %copy-start.1 = (bf16[128,4096]{1,0:T(8,128)(2,1)S(1)}, bf16[128,4096]{1,0:T(8,128)(2,1)}, u32[]{:S(2)}) copy-start(bf16[128,4096]{1,0:T(8,128)(2,1)} %get-tuple-element.46) | copy-start | bytes 3145732
  79.8 1.6 %copy-start = (bf16[128,4096]{1,0:T(8,128)(2,1)S(1)}, bf16[128,4096]{1,0:T(8,128)(2,1)}, u32[]{:S(2)}) copy-start(bf16[128,4096]{1,0:T(8,128)(2,1)} %get-tuple-element.47) | copy-start | bytes 3145732
  81.4 1.0 %copy-start.3 = (f32[128,256]{1,0:T(8,128)S(1)}, f32[128,256]{1,0:T(8,128)}, u32[]{:S(2)}) copy-start(f32[128,256]{1,0:T(8,128)} %get-tuple-element.48) | copy-start | bytes 393220

commit v3 on v2

--- a/solution.py
+++ b/solution.py
@@ -179,19 +179,13 @@
             own = slice(a * RB, (a + 1) * RB)
             mf = mf_ref[own, :]
             source = xf[a * RB : a * RB + window, col]
-            grads = xb[a * RB : a * RB + window, col]
             table = (hf[hrows, :].reshape(groups, RB, window) * mf[None]).reshape(groups * RB, window)
             conv = diagonal(jnp.dot(table, source, preferred_element_type=f32))
             pair = xf[rows + a * RB : rows + (a + 1) * RB, col]
             conv = conv + gain * pair.astype(f32)
             so_ref[own, col] = (qs[own, col] * conv).astype(bf16)
             eq[own, col] = (d_ref[own, col].astype(f32) * conv).astype(bf16)
-            table = (hb[hrows, :].reshape(groups, RB, window) * mb_ref[own, :][None]).reshape(groups * RB, window)
-            back = diagonal(jnp.dot(table, grads, preferred_element_type=f32))
             grad = xb[own, col]
-            back = back + gain * grad.astype(f32)
-            ek[own, col] = (back * vs[own, col]).astype(bf16)
-            ev[own, col] = (back * ks[own, col]).astype(bf16)
             spread = (grad[None] * lm_ref[...]).reshape(groups * RB, LANES)
             terms = lax.dot_general(
                 xf[a * RB : a * RB + reach, col], spread, (((1,), (1,)), ((), ())), preferred_element_type=f32)
@@ -216,14 +210,25 @@
                 parts[i * (groups // per) + m] = terms[m * per : (m + 1) * per, :taps]
         return carry
 
+    def pairs(i, carry):
+        col = lanes_of(i)
+        hrows = pl.ds(pl.multiple_of(i * groups * RB, groups * RB), groups * RB)
+        gain = gain_ref[0:1, col]
+        for a in range(rows // RB):
+            own = slice(a * RB, (a + 1) * RB)
+            grads = xb[a * RB : a * RB + window, col]
+            table = (hb[hrows, :].reshape(groups, RB, window) * mb_ref[own, :][None]).reshape(groups * RB, window)
+            back = diagonal(jnp.dot(table, grads, preferred_element_type=f32))
+            grad = xb[own, col]
+            back = back + gain * grad.astype(f32)
+            ek[own, col] = (back * vs[own, col]).astype(bf16)
+            ev[own, col] = (back * ks[own, col]).astype(bf16)
+        return carry
+
     for chunk in range(chunks):
         @pl.when(has_left)
         def _():
             gp_copies[chunk].wait_recv()
-
-        @pl.when(has_right)
-        def _():
-            cg_copies[chunk].wait_recv()
 
         if chunk + DEPTH < chunks:
             @pl.when(has_right)
@@ -240,10 +245,32 @@
 
         @pl.when(has_left)
         def _():
-            for copy in eb_copies[chunk]:
-                copy.start()
+            eb_copies[chunk][0].start()
 
     over_peers(lambda peer: part_copy(peer, me).start())
+
+    for chunk in range(chunks):
+        @pl.when(has_right)
+        def _():
+            cg_copies[chunk].wait_recv()
+
+        lax.fori_loop(chunk * steps, (chunk + 1) * steps, pairs, 0)
+
+        @pl.when(has_left)
+        def _():
+            eb_copies[chunk][1].start()
+            eb_copies[chunk][2].start()
+
+        if chunk == chunks // 2 - 1:
+            over_peers(lambda peer: part_copy(peer, peer).wait_recv())
+            total = parts[me]
+
+            def add(offset, total):
+                return total + inbox[peer_of(offset)]
+
+            done[me] = lax.fori_loop(1, n, add, total)
+            over_peers(lambda peer: done_copy(me, peer).start())
+
 
     def backward(slot, e_ref, out_ref, col):
         scr[slot] = e_ref[:, col].astype(f32)
@@ -268,15 +295,6 @@
                 copy.wait_recv()
 
         lax.fori_loop(chunk * steps, (chunk + 1) * steps, third, 0)
-        if chunk == chunks // 2 - 1:
-            over_peers(lambda peer: part_copy(peer, peer).wait_recv())
-            total = parts[me]
-
-            def add(offset, total):
-                return total + inbox[peer_of(offset)]
-
-            done[me] = lax.fori_loop(1, n, add, total)
-            over_peers(lambda peer: done_copy(me, peer).start())
 
     @pl.when(has_right)
     def _():

time: 83.4 us -> 84.2 us (level)
  Pallas kernels: 68.5 us -> 69.4 us
where the time goes in v3:
time: 84.2 us; the launch traced here: 83.9 us
  Pallas kernels  69.4 us (82%)
  local copies, waits for them, and re-layouts  11.3 us (13%)
  other arithmetic  2.47 us (3%)
    pallas_call x1, Pallas kernels, body(): pl.pallas_call(functools.partial(kernel, n, chunks, width, scale), out_sh...  69.4 us
    unnamed x18, local copies, waits for them, and re-layouts  8.2 us

profile of v3, /device:TPU:0, one launch (start us, length us, event | category | flops | bytes accessed | tf_op | source)
XLA Modules:
  0.0 83.9 jit_solution(14232887213308377876)
XLA Ops:
  0.6 0.0 copy-start.5
  0.7 0.7 copy-done.5
  1.3 0.1 pad_dynamic-slice_fusion
  1.4 0.1 compare_bitcast_fusion.9
  1.5 0.1 eq.108
  1.6 0.1 compare_bitcast_fusion
  1.7 0.1 stack.117
  1.7 0.1 fusion.3
  1.8 0.0 copy-start.4
  1.9 0.6 fusion.2.lm_ref
  2.5 0.2 copy-done.4
  2.7 0.1 copy.14
  2.8 0.7 fusion.1
  3.5 0.1 compare_convert_fusion
  3.6 0.2 rev.3
  3.8 0.1 pad_bitcast_fusion
  4.0 0.8 pad_maximum_fusion.base_ref
  4.8 1.1 %broadcast_in_dim.2.mshort_ref = f32[12,128,128]{2,1,0:T(8,128)} broadcast(f32[12,128]{1,0:T(8,128)S(1)} %convert_element_type.30), dimensions={0,1} | broadcast | bytes 792576 | tf_op jit(solution)/shard_map/broadcast_in_dim | solution.py:355
  5.9 0.1 tile.4
  6.1 1.2 %copy.15.mt_ref = f32[8,144,128]{2,1,0:T(8,128)} copy(f32[8,144,128]{1,2,0:T(8,128)S(1)} %bitcast.57) | data formatting | bytes 1179648 | tf_op jit(solution)/shard_map/tile | solution.py:350
  7.2 69.4 %shard_map.119 = (bf16[128,4096]{1,0:T(8,128)(2,1)}, bf16[128,4096]{1,0:T(8,128)(2,1)}, bf16[128,4096]{1,0:T(8,128)(2,1)}, bf16[128,4096]{1,0:T(8,128)(2,1)}, f32[128,256]{1,0:T(8,128)}) custom-call(bf16[128,4096]{1,0:T(8,128)(2,1)} %q_ref.1, bf16[128,4096]{1,0:T(8,128)(2,1)} %k_ref.1, bf16[128,4096]{1,0:T(8,128)(2,1)} %v_ref.1, bf16[128,4096]{1,0:T(8,128)(2,1)} %d_ref.1, ...), custom_call_target="tpu_custom_call" | custom-call | tf_op jit(solution)/shard_map/pallas_call | solution.py:368
  76.6 0.0 copy-start.2
  76.6 2.4 %copy.21 = bf16[128,4096]{1,0:T(8,128)(2,1)} copy(bf16[128,4096]{1,0:T(8,128)(2,1)} %get-tuple-element.44) | data formatting | bytes 2097152
  79.0 0.0 copy-done.2
  79.0 0.0 copy-start.1
  79.0 1.0 %copy.22 = bf16[128,4096]{1,0:T(8,128)(2,1)} copy(bf16[128,4096]{1,0:T(8,128)(2,1)S(1)} %copy-done.2) | data formatting | bytes 2097152
  80.0 0.6 copy-done.1
  80.6 1.0 %copy.23 = bf16[128,4096]{1,0:T(8,128)(2,1)} copy(bf16[128,4096]{1,0:T(8,128)(2,1)S(1)} %copy-done.1) | data formatting | bytes 2097152
  81.6 0.6 copy-done
  82.2 1.0 %copy.24 = bf16[128,4096]{1,0:T(8,128)(2,1)} copy(bf16[128,4096]{1,0:T(8,128)(2,1)S(1)} %copy-done) | data formatting | bytes 2097152
  83.2 0.1 copy-done.3
  83.2 0.7 copy.25
  (9 shorter events, 0.1 us)
Async XLA Ops:
  0.6 0.7 copy-start.5
  1.8 0.8 %copy-start.4 = (bf16[128,256]{1,0:T(8,128)(2,1)S(1)}, bf16[128,256]{1,0:T(8,128)(2,1)}, u32[]{:S(2)}) copy-start(bf16[128,256]{1,0:T(8,128)(2,1)} %param.13) | copy-start | bytes 196612
  76.6 2.4 %copy-start.2 = (bf16[128,4096]{1,0:T(8,128)(2,1)S(1)}, bf16[128,4096]{1,0:T(8,128)(2,1)}, u32[]{:S(2)}) copy-start(bf16[128,4096]{1,0:T(8,128)(2,1)} %get-tuple-element.45) | copy-start | bytes 3145732
  79.0 1.6 %copy-start.1 = (bf16[128,4096]{1,0:T(8,128)(2,1)S(1)}, bf16[128,4096]{1,0:T(8,128)(2,1)}, u32[]{:S(2)}) copy-start(bf16[128,4096]{1,0:T(8,128)(2,1)} %get-tuple-element.46) | copy-start | bytes 3145732
  80.6 1.6 %copy-start = (bf16[128,4096]{1,0:T(8,128)(2,1)S(1)}, bf16[128,4096]{1,0:T(8,128)(2,1)}, u32[]{:S(2)}) copy-start(bf16[128,4096]{1,0:T(8,128)(2,1)} %get-tuple-element.47) | copy-start | bytes 3145732
  82.2 1.0 %copy-start.3 = (f32[128,256]{1,0:T(8,128)S(1)}, f32[128,256]{1,0:T(8,128)}, u32[]{:S(2)}) copy-start(f32[128,256]{1,0:T(8,128)} %get-tuple-element.48) | copy-start | bytes 393220
